TPU v7x, 32 devices: a whole 2x2x4 slice. The times are simulated.
32 devices in a mesh: band: 4 (over y, core), grid: 8 (over z, x).
Axes of the slice: x: 2, y: 2, z: 4, core: 2. Of those that a mesh axis runs over, the one named last changes fastest.
Arguments:
- ground: float32 [4, 128, 128, 128], P('band', 'grid'), may hold values from -6 to 6
- response: float32 [4, 2, 2, 128, 128, 128], P('band', None, None, None, 'grid'), may hold values from -0.6 to 0.6
- kernel_xc: float32 [128, 128, 128], P('grid'), may hold values from -2 to -0.3
Outputs:
- applied: float32 [4, 2, 2, 128, 128, 128], P('band', None, None, None, 'grid')
All inputs are finite; a program needn't handle non-finite values.
Results may differ from a plain program's by a relative error of at most 0.0001.
Values sent between devices are 32-bit elements; how exact they have to be, the bound alone decides.
A program may use at most 64 MiB of HBM per device.

v0:
```python
import math
import jax
import jax.numpy as jnp
import numpy as np
from jax import lax
from jax.sharding import PartitionSpec as P

high = lax.Precision.HIGH
spacing = 0.4527


def dft_pair(length, direction, rows=None, columns=None):
    rows = np.arange(length) if rows is None else rows
    columns = np.arange(length) if columns is None else columns
    angles = rows[:, None] * columns[None, :] % length * (2.0 * math.pi / length)
    cosine = np.cos(angles) / math.sqrt(length)
    sine = direction * np.sin(angles) / math.sqrt(length)
    pairs = (np.stack((cosine, sine), axis=1), np.stack((-sine, cosine), axis=1))
    return np.stack(pairs, axis=0).astype(np.float32)


def ein(form, operand, table):
    return jnp.einsum(form, operand, table, precision=high)


def signed_freq(positions, length):
    return jnp.where(positions < (length + 1) // 2, positions, positions - length).astype(
        jnp.float32
    )


def coulomb(freq_first, freq_second, freq_third, length):
    squares = (
        freq_first[:, None, None] ** 2
        + freq_second[None, :, None] ** 2
        + freq_third[None, None, :] ** 2
    )
    edge_len = spacing * length
    return jnp.where(
        squares > 0.5, edge_len * edge_len / (math.pi * jnp.maximum(squares, 1.0)), 0.0
    )


def swap(values, bit, size):
    return lax.ppermute(values, "band", [(i, i ^ bit) for i in range(size)])


def hartree(density, axes, device, devices, numbers):
    length = density.shape[-1]
    forward, backward = (dft_pair(length, -1.0), dft_pair(length, 1.0))
    wave = ein("cxyz,cydk->dxkz", density, forward)
    wave = ein("dxkz,dzem->exkm", wave, forward)
    wave = lax.all_to_all(wave, axes, split_axis=2, concat_axis=1, tiled=True)
    rows = length // devices
    mine = device * rows + jnp.arange(rows, dtype=jnp.int32)
    freqs = signed_freq(jnp.arange(length, dtype=jnp.int32), length)
    weights = coulomb(freqs, signed_freq(mine, length), freqs, length)
    wave = ein("cxyz,cxdk->dkyz", wave, dft_pair(length, -1.0, rows=numbers)) * weights
    wave = ein("dkyz,dkex->exyz", wave, dft_pair(length, 1.0, columns=numbers))
    wave = lax.all_to_all(wave, axes, split_axis=1, concat_axis=2, tiled=True)
    cell = ein("dxkz,dzem->exkm", wave, backward)
    return ein("cxyz,cydk->dxkz", cell, backward)


def on_device(bands, grids, ground, response, kernel_xc):
    grid_len = ground.shape[2]
    planes = ground.shape[1]
    forward = dft_pair(grid_len, -1.0)
    backward = dft_pair(grid_len, 1.0)
    orbital = ground[0]
    flip = np.array([1.0, -1.0], np.float32)[None, None, :, None]
    partial = None
    for harmonic in range(2):
        table = backward if harmonic == 0 else backward * flip
        wave = ein("cxyz,cxdk->dkyz", response[0, harmonic], backward)
        wave = lax.all_to_all(wave, "grid", split_axis=1, concat_axis=2, tiled=True)
        wave = ein("dxkz,dzem->exkm", wave, backward)
        cell = ein("cxyz,cydk->dxkz", wave, table)
        partial = cell if partial is None else partial + cell
    partial = partial * orbital
    me_band = lax.axis_index("band")
    if planes % bands == 0 and bands & bands - 1 == 0:
        dens = partial
        kernel = kernel_xc
        bit = bands // 2
        bits = []
        while bit >= 1:
            bits.append(bit)
            bit //= 2
        steps = list(reversed(bits))
        low = jnp.int32(0)
        for bit in steps:
            half = dens.shape[1] // 2
            mine = me_band // bit % 2
            keep = lax.dynamic_slice_in_dim(dens, mine * half, half, 1)
            give = lax.dynamic_slice_in_dim(dens, (1 - mine) * half, half, 1)
            dens = keep + swap(give, bit, bands)
            low = low + mine * half
        own = dens.shape[1]
        kernel = lax.dynamic_slice_in_dim(kernel_xc, low, own, 0)
        place = [0] * bands
        for b in range(bands):
            size = planes
            for bit in steps:
                size //= 2
                place[b] += b // bit % 2 * (size // own)
        numbers = (
            np.arange(grids)[None, :, None] * planes
            + np.array(place)[:, None, None] * own
            + np.arange(own)[None, None, :]
        ).reshape(-1)
        device = me_band * grids + lax.axis_index("grid")
        pot = hartree(dens, ("band", "grid"), device, bands * grids, numbers)
        pot = pot + kernel * dens
        for bit in reversed(steps):
            mine = me_band // bit % 2
            other = swap(pot, bit, bands)
            first = jnp.where(mine == 0, pot, other)
            second = jnp.where(mine == 0, other, pot)
            pot = jnp.concatenate((first, second), axis=1)
    else:
        dens = lax.psum(partial, "band")
        pot = hartree(dens, "grid", lax.axis_index("grid"), grids, None)
        pot = pot + kernel_xc * dens
    prod = pot * orbital
    outs = []
    for harmonic in range(2):
        table = forward if harmonic == 0 else forward * flip.reshape(2, 1, 1, 1)
        wave = ein("cxyz,cydk->dxkz", prod, table)
        wave = ein("dxkz,dzem->exkm", wave, forward)
        wave = lax.all_to_all(wave, "grid", split_axis=2, concat_axis=1, tiled=True)
        outs.append(ein("cxyz,cxdk->dkyz", wave, forward))
    return jnp.stack(outs, axis=0)[None]


def solution(mesh):
    bands, grids = (mesh.shape["band"], mesh.shape["grid"])

    def body(ground, response, kernel_xc):
        return on_device(bands, grids, ground, response, kernel_xc)

    return jax.shard_map(
        body,
        mesh=mesh,
        in_specs=(
            P("band", "grid", None, None),
            P("band", None, None, None, "grid", None),
            P("grid", None, None),
        ),
        out_specs=P("band", None, None, None, "grid", None),
        check_vma=False,
    )
```

profile of v0, /device:TPU:0, one launch (start us, length us, event | category | flops | bytes accessed | tf_op | source)
XLA Modules:
  0.0 335.6 jit_solution(17473547233296567763)
XLA Ops:
  0.0 4.0 %fusion.46 = (f32[1,1,2,128,16,128]{5,4,3,2,1,0:T(8,128)S(1)}, f32[1,1,2,128,16,128]{5,4,3,2,1,0:T(8,128)}) fusion(f32[1,2,2,128,16,128]{5,4,3,2,1,0:T(8,128)} %param.22), kind=kLoop, calls=%fused_computation.68 | loop fusion | bytes 8388608 | tf_op jit(solution)/shard_map/slice | solution.py:75
  4.1 1.6 fusion.23
  5.7 2.5 copy.81
  8.2 7.3 %all-to-all-start = ((f32[2,128,16,128]{3,2,0,1:T(8,128)}), f32[2,128,16,128]{3,2,0,1:T(8,128)}, u32[]{:S(2)}, u32[]{:S(2)}) async-start(f32[2,128,16,128]{3,2,0,1:T(8,128)} %copy.81), calls=%async_computation | async-start | bytes 4194304 | tf_op jit(solution)/shard_map/all_to_all | solution.py:76
  15.5 3.2 fusion.24
  18.6 2.5 copy.89
  21.2 42.6 %all-to-all-done = f32[2,128,16,128]{3,2,0,1:T(8,128)} async-done(((f32[2,128,16,128]{3,2,0,1:T(8,128)}), f32[2,128,16,128]{3,2,0,1:T(8,128)}, u32[]{:S(2)}, u32[]{:S(2)}) %all-to-all-start) | async-done | bytes 2097184 | tf_op jit(solution)/shard_map/all_to_all | solution.py:76
  63.8 4.5 %all-to-all-start.1 = ((f32[2,128,16,128]{3,2,0,1:T(8,128)}), f32[2,128,16,128]{3,2,0,1:T(8,128)}, u32[]{:S(2)}, u32[]{:S(2)}) async-start(f32[2,128,16,128]{3,2,0,1:T(8,128)} %copy.89), calls=%async_computation.1 | async-start | bytes 4194304 | tf_op jit(solution)/shard_map/all_to_all | solution.py:76
  68.4 0.3 copy.95
  68.7 3.2 copy.83
  72.0 44.1 %all-to-all-done.1 = f32[2,128,16,128]{3,2,0,1:T(8,128)} async-done(((f32[2,128,16,128]{3,2,0,1:T(8,128)}), f32[2,128,16,128]{3,2,0,1:T(8,128)}, u32[]{:S(2)}, u32[]{:S(2)}) %all-to-all-start.1) | async-done | bytes 2097184 | tf_op jit(solution)/shard_map/all_to_all | solution.py:76
  116.1 2.0 copy.91
  118.1 0.2 copy-done.2
  118.3 1.0 fusion.13
  119.4 1.0 fusion.11
  120.4 1.9 fusion.7
  122.3 1.9 bitcast_multiply_fusion
  124.2 1.3 copy-done.4
  125.7 2.7 collective-permute-done
  128.5 1.7 dynamic-slice_add_fusion
  130.1 0.8 constant_dynamic-slice_fusion.1
  131.0 1.5 collective-permute-start.1
  132.5 12.8 %collective-permute-done.1 = f32[2,4,128,128]{2,3,0,1:T(8,128)} collective-permute-done((f32[2,4,128,128]{2,3,0,1:T(8,128)}, f32[2,4,128,128]{2,3,0,1:T(8,128)}, u32[]{:S(2)}, u32[]{:S(2)}) %collective-permute-start.1) | collective-permute-done | bytes 524320 | tf_op jit(solution)/shard_map/ppermute | solution.py:45
  145.2 1.4 convolution_bitcast_fusion.7
  146.7 0.6 convolution_bitcast_fusion.6
  147.3 1.2 copy.97
  148.5 3.7 %all-to-all-start.2 = ((f32[2,4,128,128]{3,0,1,2:T(2,128)}), f32[2,4,128,128]{3,0,1,2:T(2,128)}, u32[]{:S(2)}, u32[]{:S(2)}) async-start(f32[2,4,128,128]{3,0,1,2:T(2,128)} %copy.97), calls=%async_computation.2 | async-start | bytes 1048576 | tf_op jit(solution)/shard_map/all_to_all | solution.py:53
  152.3 0.9 fusion.38
  153.2 15.4 %all-to-all-done.2 = f32[2,4,128,128]{3,0,1,2:T(2,128)} async-done(((f32[2,4,128,128]{3,0,1,2:T(2,128)}), f32[2,4,128,128]{3,0,1,2:T(2,128)}, u32[]{:S(2)}, u32[]{:S(2)}) %all-to-all-start.2) | async-done | bytes 524320 | tf_op jit(solution)/shard_map/all_to_all | solution.py:53
  168.5 1.2 copy.98
  169.8 1.4 fusion.30
  171.2 0.4 convolution_bitcast_fusion.4
  171.6 1.1 copy.100
  172.7 3.6 %all-to-all-start.3 = ((f32[2,128,4,128]{3,2,0,1:T(4,128)}), f32[2,128,4,128]{3,2,0,1:T(4,128)}, u32[]{:S(2)}, u32[]{:S(2)}) async-start(f32[2,128,4,128]{3,2,0,1:T(4,128)} %copy.100), calls=%async_computation.3 | async-start | bytes 1048576 | tf_op jit(solution)/shard_map/all_to_all | solution.py:60
  176.3 0.7 constant_dynamic-slice_fusion
  177.0 1.1 copy.106
  178.2 14.2 %all-to-all-done.3 = f32[2,128,4,128]{3,2,0,1:T(4,128)} async-done(((f32[2,128,4,128]{3,2,0,1:T(4,128)}), f32[2,128,4,128]{3,2,0,1:T(4,128)}, u32[]{:S(2)}, u32[]{:S(2)}) %all-to-all-start.3) | async-done | bytes 524320 | tf_op jit(solution)/shard_map/all_to_all | solution.py:60
  192.4 1.1 copy.101
  193.5 1.4 convolution_bitcast_fusion.3
  194.9 1.7 multiply_add_fusion
  196.6 0.6 collective-permute-start.2
  197.2 0.2 copy-done.10
  197.4 12.5 %collective-permute-done.2 = f32[2,4,128,128]{2,3,0,1:T(8,128)S(1)} collective-permute-done((f32[2,4,128,128]{2,3,0,1:T(8,128)S(1)}, f32[2,4,128,128]{2,3,0,1:T(8,128)S(1)}, u32[]{:S(2)}, u32[]{:S(2)}) %collective-permute-start.2) | collective-permute-done | bytes 524320 | tf_op jit(solution)/shard_map/ppermute | solution.py:45
  209.9 1.1 broadcast_select_fusion.3
  211.2 0.6 copy-done.8
  212.0 2.0 collective-permute-done.3
  214.0 1.7 broadcast_select_fusion.1
  215.7 1.0 fusion.25
  216.7 1.9 fusion.20
  218.6 2.9 copy.112
  221.5 4.3 %all-to-all-start.5 = ((f32[2,16,128,128]{3,0,1,2:T(2,128)}), f32[2,16,128,128]{3,0,1,2:T(2,128)}, u32[]{:S(2)}, u32[]{:S(2)}) async-start(f32[2,16,128,128]{3,0,1,2:T(2,128)} %copy.112), calls=%async_computation.5 | async-start | bytes 4194304 | tf_op jit(solution)/shard_map/all_to_all | solution.py:131
  225.9 1.0 fusion.27
  226.9 1.9 fusion.17
  228.7 2.9 copy.108
  231.7 43.0 %all-to-all-done.5 = f32[2,16,128,128]{3,0,1,2:T(2,128)} async-done(((f32[2,16,128,128]{3,0,1,2:T(2,128)}), f32[2,16,128,128]{3,0,1,2:T(2,128)}, u32[]{:S(2)}, u32[]{:S(2)}) %all-to-all-start.5) | async-done | bytes 2097184 | tf_op jit(solution)/shard_map/all_to_all | solution.py:131
  274.7 3.9 %all-to-all-start.4 = ((f32[2,16,128,128]{3,0,1,2:T(2,128)}), f32[2,16,128,128]{3,0,1,2:T(2,128)S(1)}, u32[]{:S(2)}, u32[]{:S(2)}) async-start(f32[2,16,128,128]{3,0,1,2:T(2,128)} %copy.108), calls=%async_computation.4 | async-start | bytes 4194304 | tf_op jit(solution)/shard_map/all_to_all | solution.py:131
  278.5 3.2 copy.113
  281.7 45.1 %all-to-all-done.4 = f32[2,16,128,128]{3,0,1,2:T(2,128)S(1)} async-done(((f32[2,16,128,128]{3,0,1,2:T(2,128)}), f32[2,16,128,128]{3,0,1,2:T(2,128)S(1)}, u32[]{:S(2)}, u32[]{:S(2)}) %all-to-all-start.4) | async-done | bytes 2097184 | tf_op jit(solution)/shard_map/all_to_all | solution.py:131
  326.8 0.2 copy.109
  327.1 1.3 copy-done.3
  328.4 1.2 convolution_bitcast_fusion
  329.6 1.2 convolution_bitcast_fusion.1
  330.8 0.4 maximum_bitcast_fusion
  331.2 4.4 %copy.115 = f32[1,2,2,128,16,128]{5,4,3,2,1,0:T(8,128)} copy(f32[1,2,2,128,16,128]{5,3,4,2,1,0:T(8,128)S(1)} %maximum_bitcast_fusion) | data formatting | bytes 8388608 | tf_op jit(solution)/shard_map/broadcast_in_dim | solution.py:133
  (36 shorter events, 0.6 us)
Async XLA Ops:
  0.0 176.3 %copy-start = (f32[16,128,128]{2,1,0:T(8,128)S(1)}, f32[16,128,128]{2,1,0:T(8,128)}, u32[]{:S(2)}) copy-start(f32[16,128,128]{2,1,0:T(8,128)} %param.23) | copy-start | bytes 3145732
  0.0 4.0 %copy-start.12 = (f32[2,128,2,128,1]{1,3,0,4,2:T(8,128)S(1)}, f32[2,128,2,128,1]{1,3,0,4,2:T(8,128)}, u32[]{:S(2)}) copy-start(f32[2,128,2,128,1]{1,3,0,4,2:T(8,128)} %constant.98) | copy-start | bytes 786436
  8.2 55.6 %all-to-all-start = ((f32[2,128,16,128]{3,2,0,1:T(8,128)}), f32[2,128,16,128]{3,2,0,1:T(8,128)}, u32[]{:S(2)}, u32[]{:S(2)}) async-start(f32[2,128,16,128]{3,2,0,1:T(8,128)} %copy.81), calls=%async_computation | async-start | bytes 4194304 | tf_op jit(solution)/shard_map/all_to_all | solution.py:76
  21.2 47.2 %copy-start.13 = (f32[1,16,128,128]{3,2,1,0:T(8,128)S(1)}, f32[1,16,128,128]{3,2,1,0:T(8,128)}, u32[]{:S(2)}) copy-start(f32[1,16,128,128]{3,2,1,0:T(8,128)} %param.21) | copy-start | bytes 3145732
  63.8 52.3 %all-to-all-start.1 = ((f32[2,128,16,128]{3,2,0,1:T(8,128)}), f32[2,128,16,128]{3,2,0,1:T(8,128)}, u32[]{:S(2)}, u32[]{:S(2)}) async-start(f32[2,128,16,128]{3,2,0,1:T(8,128)} %copy.89), calls=%async_computation.1 | async-start | bytes 4194304 | tf_op jit(solution)/shard_map/all_to_all | solution.py:76
  116.1 2.2 copy-start.2
  116.1 2.2 copy-start.6
  119.3 1.1 copy-start.14
  124.2 1.3 copy-start.4
  125.6 2.9 collective-permute-start
  125.7 19.5 %copy-start.5 = (f32[2,128,2,128,1]{3,1,0,2,4:T(8,128)S(1)}, f32[2,128,2,128,1]{3,1,0,2,4:T(8,128)}, u32[]{:S(2)}) copy-start(f32[2,128,2,128,1]{3,1,0,2,4:T(8,128)} %constant.101) | copy-start | bytes 786436
  131.0 14.3 %collective-permute-start.1 = (f32[2,4,128,128]{2,3,0,1:T(8,128)}, f32[2,4,128,128]{2,3,0,1:T(8,128)}, u32[]{:S(2)}, u32[]{:S(2)}) collective-permute-start(f32[2,4,128,128]{2,3,0,1:T(8,128)} %constant_dynamic-slice_fusion.1), channel_id=1, source_target_pairs={{0,16},{8,24},{16,0},{24,8},{1,17},{9,25},{17,1},{25,9},{2,18},{10... | collective-permute-start | bytes 1572872 | tf_op jit(solution)/shard_map/ppermute | solution.py:45
  148.5 20.0 %all-to-all-start.2 = ((f32[2,4,128,128]{3,0,1,2:T(2,128)}), f32[2,4,128,128]{3,0,1,2:T(2,128)}, u32[]{:S(2)}, u32[]{:S(2)}) async-start(f32[2,4,128,128]{3,0,1,2:T(2,128)} %copy.97), calls=%async_computation.2 | async-start | bytes 1048576 | tf_op jit(solution)/shard_map/all_to_all | solution.py:53
  168.5 2.7 copy-start.16
  172.7 19.7 %all-to-all-start.3 = ((f32[2,128,4,128]{3,2,0,1:T(4,128)}), f32[2,128,4,128]{3,2,0,1:T(4,128)}, u32[]{:S(2)}, u32[]{:S(2)}) async-start(f32[2,128,4,128]{3,2,0,1:T(4,128)} %copy.100), calls=%async_computation.3 | async-start | bytes 1048576 | tf_op jit(solution)/shard_map/all_to_all | solution.py:60
  177.0 17.9 %copy-start.7 = (f32[2,128,2,128,1]{1,3,0,2,4:T(8,128)S(1)}, f32[2,128,2,128,1]{1,3,0,2,4:T(8,128)}, u32[]{:S(2)}) copy-start(f32[2,128,2,128,1]{1,3,0,2,4:T(8,128)} %constant.99) | copy-start | bytes 786436
  196.6 0.8 copy-start.10
  196.6 13.3 %collective-permute-start.2 = (f32[2,4,128,128]{2,3,0,1:T(8,128)S(1)}, f32[2,4,128,128]{2,3,0,1:T(8,128)S(1)}, u32[]{:S(2)}, u32[]{:S(2)}) collective-permute-start(f32[2,4,128,128]{2,3,0,1:T(8,128)S(1)} %multiply_add_fusion), channel_id=1, source_target_pairs={{0,16},{8,24},{16,0},{24,8},{1,17},{9,25},{17,1},{25,9},{2,18},{10... | collective-permute-start | bytes 1572872 | tf_op jit(solution)/shard_map/ppermute | solution.py:45
  211.0 0.8 copy-start.8
  211.0 1.0 copy-start.9
  211.1 2.9 collective-permute-start.3
  212.0 3.7 %copy-start.15 = (f32[2,128,2,128,1]{3,1,0,2,4:T(8,128)S(1)}, f32[2,128,2,128,1]{3,1,0,2,4:T(8,128)}, u32[]{:S(2)}) copy-start(f32[2,128,2,128,1]{3,1,0,2,4:T(8,128)} %constant.100) | copy-start | bytes 786436
  221.5 53.2 %all-to-all-start.5 = ((f32[2,16,128,128]{3,0,1,2:T(2,128)}), f32[2,16,128,128]{3,0,1,2:T(2,128)}, u32[]{:S(2)}, u32[]{:S(2)}) async-start(f32[2,16,128,128]{3,0,1,2:T(2,128)} %copy.112), calls=%async_computation.5 | async-start | bytes 4194304 | tf_op jit(solution)/shard_map/all_to_all | solution.py:131
  274.7 52.1 %all-to-all-start.4 = ((f32[2,16,128,128]{3,0,1,2:T(2,128)}), f32[2,16,128,128]{3,0,1,2:T(2,128)S(1)}, u32[]{:S(2)}, u32[]{:S(2)}) async-start(f32[2,16,128,128]{3,0,1,2:T(2,128)} %copy.108), calls=%async_computation.4 | async-start | bytes 4194304 | tf_op jit(solution)/shard_map/all_to_all | solution.py:131
  326.8 1.6 copy-start.3
  326.8 1.6 copy-start.11
  331.2 4.5 %copy-start.1 = (f32[16,128,128]{2,1,0:T(8,128)S(1)}, f32[16,128,128]{2,1,0:T(8,128)}, u32[]{:S(2)}) copy-start(f32[16,128,128]{2,1,0:T(8,128)} %param.23) | copy-start | bytes 3145732
where the time goes:
time: 337 us; the launch traced here: 336 us
  waiting for transfers between devices  234 us (69%)
  local copies, waits for them, and re-layouts  39.8 us (12%)
  starting transfers between devices  29.5 us (9%)
  matrix products  25.6 us (8%)
  other arithmetic  5.86 us (2%)
    all_to_all x2, waiting for transfers between devices, on_device(): wave = lax.all_to_all(wave, 'grid', split_axis=2, concat_axis=1, tiled=True)  88.1 us
    all_to_all x2, waiting for transfers between devices, on_device(): wave = lax.all_to_all(wave, 'grid', split_axis=1, concat_axis=2, tiled=True)  86.7 us
    ppermute x4, waiting for transfers between devices, swap(): return lax.ppermute(values, 'band', [(i, i ^ bit) for i in range(size)])  29.9 us
    dot_general x18, matrix products, ein(): return jnp.einsum(form, operand, table, precision=high)  25.6 us
    all_to_all x1, waiting for transfers between devices, hartree(): wave = lax.all_to_all(wave, axes, split_axis=2, concat_axis=1, tiled=True)  15.4 us
    all_to_all x1, waiting for transfers between devices, hartree(): wave = lax.all_to_all(wave, axes, split_axis=1, concat_axis=2, tiled=True)  14.2 us
    all_to_all x2, starting transfers between devices, on_device(): wave = lax.all_to_all(wave, 'grid', split_axis=1, concat_axis=2, tiled=True)  11.8 us
    all_to_all x2, starting transfers between devices, on_device(): wave = lax.all_to_all(wave, 'grid', split_axis=2, concat_axis=1, tiled=True)  8.2 us
  transfers between devices with their start and end apart: 10, of which 10 were waited for; matrix products, arithmetic and copies ran while one was open for 6% of the time, Pallas kernels for 0%

commit v1 on v0

--- a/solution.py
+++ b/solution.py
@@ -7,6 +7,22 @@
 
 high = lax.Precision.HIGH
 spacing = 0.4527
+
+
+def exchange_in_pairs(value, axis, split, join):
+    ways, here = (lax.axis_size(axis), lax.axis_index(axis))
+    width = value.shape[split] // ways
+    shape = list(value.shape)
+    shape[split] = width
+    height = shape[join]
+    shape[join] = height * ways
+    full = jnp.zeros(shape, value.dtype)
+    for mask in range(ways):
+        part = lax.dynamic_slice_in_dim(value, (here ^ mask) * width, width, axis=split)
+        if mask:
+            part = lax.ppermute(part, axis, [(d, d ^ mask) for d in range(ways)])
+        full = lax.dynamic_update_slice_in_dim(full, part, (here ^ mask) * height, axis=join)
+    return full
 
 
 def dft_pair(length, direction, rows=None, columns=None):
@@ -128,7 +144,7 @@
         table = forward if harmonic == 0 else forward * flip.reshape(2, 1, 1, 1)
         wave = ein("cxyz,cydk->dxkz", prod, table)
         wave = ein("dxkz,dzem->exkm", wave, forward)
-        wave = lax.all_to_all(wave, "grid", split_axis=2, concat_axis=1, tiled=True)
+        wave = exchange_in_pairs(wave, "grid", 2, 1)
         outs.append(ein("cxyz,cxdk->dkyz", wave, forward))
     return jnp.stack(outs, axis=0)[None]
 

time: 337 us -> 322 us (0.955)
  the two profiles are of different devices: /device:TPU:0 before, /device:TPU:8 now
where the time goes in v1:
time: 322 us; the launch traced here: 321 us
  waiting for transfers between devices  210 us (65%)
  starting transfers between devices  47 us (15%)
  local copies, waits for them, and re-layouts  32.1 us (10%)
  matrix products  25.5 us (8%)
  other arithmetic  5.63 us (2%)
    all_to_all x2, waiting for transfers between devices, on_device(): wave = lax.all_to_all(wave, 'grid', split_axis=1, concat_axis=2, tiled=True)  81.6 us
    ppermute x14, waiting for transfers between devices, exchange_in_pairs(): part = lax.ppermute(part, axis, [(d, d ^ mask) for d in range(ways)])  69 us
    ppermute x4, waiting for transfers between devices, swap(): return lax.ppermute(values, 'band', [(i, i ^ bit) for i in range(size)])  31.7 us
    dot_general x18, matrix products, ein(): return jnp.einsum(form, operand, table, precision=high)  25.5 us
    ppermute x14, starting transfers between devices, exchange_in_pairs(): part = lax.ppermute(part, axis, [(d, d ^ mask) for d in range(ways)])  20.9 us
    all_to_all x1, waiting for transfers between devices, hartree(): wave = lax.all_to_all(wave, axes, split_axis=2, concat_axis=1, tiled=True)  14.4 us
    all_to_all x1, waiting for transfers between devices, hartree(): wave = lax.all_to_all(wave, axes, split_axis=1, concat_axis=2, tiled=True)  13.3 us
    all_to_all x2, starting transfers between devices, on_device(): wave = lax.all_to_all(wave, 'grid', split_axis=1, concat_axis=2, tiled=True)  13.1 us
  transfers between devices with their start and end apart: 22, of which 17 were waited for; matrix products, arithmetic and copies ran while one was open for 6% of the time, Pallas kernels for 0%

profile of v1, /device:TPU:8, one launch (start us, length us, event | category | flops | bytes accessed | tf_op | source)
XLA Modules:
  0.0 320.9 jit_solution(5289235824450186333)
XLA Ops:
  0.0 4.0 %fusion.56 = (f32[1,1,2,128,16,128]{5,4,3,2,1,0:T(8,128)}, f32[1,1,2,128,16,128]{5,4,3,2,1,0:T(8,128)S(1)}) fusion(f32[1,2,2,128,16,128]{5,4,3,2,1,0:T(8,128)} %param.22), kind=kLoop, calls=%fused_computation.104 | loop fusion | bytes 8388608 | tf_op jit(solution)/shard_map/slice | solution.py:91
  4.1 1.6 fusion.34
  5.7 2.6 copy.129
  8.3 6.3 %all-to-all-start.1 = ((f32[2,128,16,128]{3,2,0,1:T(8,128)}), f32[2,128,16,128]{3,2,0,1:T(8,128)}, u32[]{:S(2)}, u32[]{:S(2)}) async-start(f32[2,128,16,128]{3,2,0,1:T(8,128)} %copy.129), calls=%async_computation.1 | async-start | bytes 4194304 | tf_op jit(solution)/shard_map/all_to_all | solution.py:92
  14.5 3.2 fusion.33
  17.7 2.5 copy.121
  20.2 40.1 %all-to-all-done.1 = f32[2,128,16,128]{3,2,0,1:T(8,128)} async-done(((f32[2,128,16,128]{3,2,0,1:T(8,128)}), f32[2,128,16,128]{3,2,0,1:T(8,128)}, u32[]{:S(2)}, u32[]{:S(2)}) %all-to-all-start.1) | async-done | bytes 2097184 | tf_op jit(solution)/shard_map/all_to_all | solution.py:92
  60.3 6.8 %all-to-all-start = ((f32[2,128,16,128]{3,2,0,1:T(8,128)}), f32[2,128,16,128]{3,2,0,1:T(8,128)}, u32[]{:S(2)}, u32[]{:S(2)}) async-start(f32[2,128,16,128]{3,2,0,1:T(8,128)} %copy.121), calls=%async_computation | async-start | bytes 4194304 | tf_op jit(solution)/shard_map/all_to_all | solution.py:92
  67.5 3.2 copy.131
  70.6 41.5 %all-to-all-done = f32[2,128,16,128]{3,2,0,1:T(8,128)} async-done(((f32[2,128,16,128]{3,2,0,1:T(8,128)}), f32[2,128,16,128]{3,2,0,1:T(8,128)}, u32[]{:S(2)}, u32[]{:S(2)}) %all-to-all-start) | async-done | bytes 2097184 | tf_op jit(solution)/shard_map/all_to_all | solution.py:92
  112.2 2.0 copy.123
  114.4 1.0 fusion.15
  115.4 1.0 fusion.17
  116.5 1.9 fusion.7
  118.3 1.9 bitcast_multiply_fusion
  120.3 1.3 copy-done.3
  121.8 2.7 collective-permute-done
  124.6 1.7 dynamic-slice_add_fusion
  126.2 0.8 constant_dynamic-slice_fusion.1
  127.0 1.5 collective-permute-start.1
  128.6 12.8 %collective-permute-done.1 = f32[2,4,128,128]{2,3,0,1:T(8,128)} collective-permute-done((f32[2,4,128,128]{2,3,0,1:T(8,128)}, f32[2,4,128,128]{2,3,0,1:T(8,128)}, u32[]{:S(2)}, u32[]{:S(2)}) %collective-permute-start.1) | collective-permute-done | bytes 524320 | tf_op jit(solution)/shard_map/ppermute | solution.py:61
  141.3 1.4 convolution_bitcast_fusion.5
  143.4 1.2 copy.137
  144.6 6.4 %all-to-all-start.2 = ((f32[2,4,128,128]{3,0,1,2:T(2,128)}), f32[2,4,128,128]{3,0,1,2:T(2,128)}, u32[]{:S(2)}, u32[]{:S(2)}) async-start(f32[2,4,128,128]{3,0,1,2:T(2,128)} %copy.137), calls=%async_computation.2 | async-start | bytes 1048576 | tf_op jit(solution)/shard_map/all_to_all | solution.py:69
  151.1 0.8 fusion.48
  151.9 14.4 %all-to-all-done.2 = f32[2,4,128,128]{3,0,1,2:T(2,128)} async-done(((f32[2,4,128,128]{3,0,1,2:T(2,128)}), f32[2,4,128,128]{3,0,1,2:T(2,128)}, u32[]{:S(2)}, u32[]{:S(2)}) %all-to-all-start.2) | async-done | bytes 524320 | tf_op jit(solution)/shard_map/all_to_all | solution.py:69
  166.3 1.2 copy.138
  167.5 1.4 fusion.40
  169.3 1.1 copy.140
  170.4 4.5 %all-to-all-start.3 = ((f32[2,128,4,128]{3,2,0,1:T(4,128)}), f32[2,128,4,128]{3,2,0,1:T(4,128)}, u32[]{:S(2)}, u32[]{:S(2)}) async-start(f32[2,128,4,128]{3,2,0,1:T(4,128)} %copy.140), calls=%async_computation.3 | async-start | bytes 1048576 | tf_op jit(solution)/shard_map/all_to_all | solution.py:76
  175.0 0.7 constant_dynamic-slice_fusion
  175.7 1.1 copy.146
  176.8 13.3 %all-to-all-done.3 = f32[2,128,4,128]{3,2,0,1:T(4,128)} async-done(((f32[2,128,4,128]{3,2,0,1:T(4,128)}), f32[2,128,4,128]{3,2,0,1:T(4,128)}, u32[]{:S(2)}, u32[]{:S(2)}) %all-to-all-start.3) | async-done | bytes 524320 | tf_op jit(solution)/shard_map/all_to_all | solution.py:76
  190.1 1.1 copy.141
  191.3 1.4 convolution_bitcast_fusion.1
  192.6 1.7 multiply_add_fusion
  194.9 13.5 %collective-permute-done.2 = f32[2,4,128,128]{2,3,0,1:T(8,128)} collective-permute-done((f32[2,4,128,128]{2,3,0,1:T(8,128)S(1)}, f32[2,4,128,128]{2,3,0,1:T(8,128)}, u32[]{:S(2)}, u32[]{:S(2)}) %collective-permute-start.2) | collective-permute-done | bytes 524320 | tf_op jit(solution)/shard_map/ppermute | solution.py:61
  208.4 1.1 broadcast_select_fusion.3
  209.8 2.7 collective-permute-done.3
  212.5 1.4 broadcast_select_fusion.1
  213.9 1.0 fusion.37
  214.9 1.0 fusion.35
  215.9 1.9 fusion.27
  218.2 2.2 collective-permute-start.5
  220.3 1.3 collective-permute-start.6
  221.7 0.7 collective-permute-start.7
  222.4 1.8 collective-permute-start.8
  224.2 1.9 fusion.30
  228.0 7.6 %collective-permute-done.5 = f32[2,16,16,128]{3,2,0,1:T(8,128)S(1)} collective-permute-done((f32[2,16,16,128]{3,2,0,1:T(8,128)S(1)}, f32[2,16,16,128]{3,2,0,1:T(8,128)S(1)}, u32[]{:S(2)}, u32[]{:S(2)}) %collective-permute-start.5) | collective-permute-done | bytes 262176 | tf_op jit(solution)/shard_map/ppermute | solution.py:23
  235.6 2.0 collective-permute-start.10
  237.8 2.3 collective-permute-done.6
  240.2 4.0 %collective-permute-start.12 = (f32[2,16,16,128]{3,2,0,1:T(8,128)S(1)}, f32[2,16,16,128]{3,2,0,1:T(8,128)S(1)}, u32[]{:S(2)}, u32[]{:S(2)}) collective-permute-start(f32[2,16,16,128]{3,2,0,1:T(8,128)S(1)} %get-tuple-element.20), channel_id=1, source_target_pairs={{0,2},{1,3},{2,0},{3,1},{4,6},{5,7},{6,4},{7,5},{8,10},{9,11},{10,... | collective-permute-start | bytes 786440 | tf_op jit(solution)/shard_map/ppermute | solution.py:23
  244.4 12.8 %collective-permute-done.8 = f32[2,16,16,128]{3,2,0,1:T(8,128)S(1)} collective-permute-done((f32[2,16,16,128]{3,2,0,1:T(8,128)S(1)}, f32[2,16,16,128]{3,2,0,1:T(8,128)S(1)}, u32[]{:S(2)}, u32[]{:S(2)}) %collective-permute-start.8) | collective-permute-done | bytes 262176 | tf_op jit(solution)/shard_map/ppermute | solution.py:23
  257.3 4.2 %collective-permute-start.13 = (f32[2,16,16,128]{3,2,0,1:T(8,128)S(1)}, f32[2,16,16,128]{3,2,0,1:T(8,128)S(1)}, u32[]{:S(2)}, u32[]{:S(2)}) collective-permute-start(f32[2,16,16,128]{3,2,0,1:T(8,128)S(1)} %get-tuple-element.19), channel_id=1, source_target_pairs={{0,3},{1,2},{2,1},{3,0},{4,7},{5,6},{6,5},{7,4},{8,11},{9,10},{10,... | collective-permute-start | bytes 786440 | tf_op jit(solution)/shard_map/ppermute | solution.py:23
  261.6 3.1 collective-permute-done.9
  264.8 12.2 %collective-permute-done.10 = f32[2,16,16,128]{3,2,0,1:T(8,128)S(1)} collective-permute-done((f32[2,16,16,128]{3,2,0,1:T(8,128)S(1)}, f32[2,16,16,128]{3,2,0,1:T(8,128)S(1)}, u32[]{:S(2)}, u32[]{:S(2)}) %collective-permute-start.10) | collective-permute-done | bytes 262176 | tf_op jit(solution)/shard_map/ppermute | solution.py:23
  277.2 1.2 fusion.19
  278.4 3.9 %collective-permute-start.16 = (f32[2,16,16,128]{3,2,0,1:T(8,128)S(1)}, f32[2,16,16,128]{3,2,0,1:T(8,128)S(1)}, u32[]{:S(2)}, u32[]{:S(2)}) collective-permute-start(f32[2,16,16,128]{3,2,0,1:T(8,128)S(1)} %get-tuple-element.16), channel_id=1, source_target_pairs={{0,6},{1,7},{2,4},{3,5},{4,2},{5,3},{6,0},{7,1},{8,14},{9,15},{10,... | collective-permute-start | bytes 786440 | tf_op jit(solution)/shard_map/ppermute | solution.py:23
  283.2 13.5 %collective-permute-done.14 = f32[2,16,16,128]{3,2,0,1:T(8,128)S(1)} collective-permute-done((f32[2,16,16,128]{3,2,0,1:T(8,128)S(1)}, f32[2,16,16,128]{3,2,0,1:T(8,128)S(1)}, u32[]{:S(2)}, u32[]{:S(2)}) %collective-permute-start.14) | collective-permute-done | bytes 262176 | tf_op jit(solution)/shard_map/ppermute | solution.py:23
  296.9 5.5 %collective-permute-done.15 = f32[2,16,16,128]{3,2,0,1:T(8,128)S(1)} collective-permute-done((f32[2,16,16,128]{3,2,0,1:T(8,128)S(1)}, f32[2,16,16,128]{3,2,0,1:T(8,128)S(1)}, u32[]{:S(2)}, u32[]{:S(2)}) %collective-permute-start.15) | collective-permute-done | bytes 262176 | tf_op jit(solution)/shard_map/ppermute | solution.py:23
  302.5 7.1 %collective-permute-done.16 = f32[2,16,16,128]{3,2,0,1:T(8,128)S(1)} collective-permute-done((f32[2,16,16,128]{3,2,0,1:T(8,128)S(1)}, f32[2,16,16,128]{3,2,0,1:T(8,128)S(1)}, u32[]{:S(2)}, u32[]{:S(2)}) %collective-permute-start.16) | collective-permute-done | bytes 262176 | tf_op jit(solution)/shard_map/ppermute | solution.py:23
  309.8 4.8 %collective-permute-done.17 = f32[2,16,16,128]{3,2,0,1:T(8,128)S(1)} collective-permute-done((f32[2,16,16,128]{3,2,0,1:T(8,128)S(1)}, f32[2,16,16,128]{3,2,0,1:T(8,128)S(1)}, u32[]{:S(2)}, u32[]{:S(2)}) %collective-permute-start.17) | collective-permute-done | bytes 262176 | tf_op jit(solution)/shard_map/ppermute | solution.py:23
  314.9 1.1 fusion.22
  316.5 4.4 %copy.167 = f32[1,2,2,128,16,128]{5,4,3,2,1,0:T(8,128)} copy(f32[1,2,2,128,16,128]{5,3,4,2,1,0:T(8,128)S(1)} %maximum_bitcast_fusion) | data formatting | bytes 8388608 | tf_op jit(solution)/shard_map/broadcast_in_dim | solution.py:149
  (68 shorter events, 7.8 us)
Async XLA Ops:
  0.0 174.9 %copy-start = (f32[16,128,128]{2,1,0:T(8,128)S(1)}, f32[16,128,128]{2,1,0:T(8,128)}, u32[]{:S(2)}) copy-start(f32[16,128,128]{2,1,0:T(8,128)} %param.23) | copy-start | bytes 3145732
  0.0 4.1 %copy-start.8 = (f32[2,128,2,128,1]{1,3,0,4,2:T(8,128)S(1)}, f32[2,128,2,128,1]{1,3,0,4,2:T(8,128)}, u32[]{:S(2)}) copy-start(f32[2,128,2,128,1]{1,3,0,4,2:T(8,128)} %constant.109) | copy-start | bytes 786436
  8.3 52.0 %all-to-all-start.1 = ((f32[2,128,16,128]{3,2,0,1:T(8,128)}), f32[2,128,16,128]{3,2,0,1:T(8,128)}, u32[]{:S(2)}, u32[]{:S(2)}) async-start(f32[2,128,16,128]{3,2,0,1:T(8,128)} %copy.129), calls=%async_computation.1 | async-start | bytes 4194304 | tf_op jit(solution)/shard_map/all_to_all | solution.py:92
  20.2 46.9 %copy-start.9 = (f32[1,16,128,128]{3,2,1,0:T(8,128)S(1)}, f32[1,16,128,128]{3,2,1,0:T(8,128)}, u32[]{:S(2)}) copy-start(f32[1,16,128,128]{3,2,1,0:T(8,128)} %param.21) | copy-start | bytes 3145732
  60.3 51.9 %all-to-all-start = ((f32[2,128,16,128]{3,2,0,1:T(8,128)}), f32[2,128,16,128]{3,2,0,1:T(8,128)}, u32[]{:S(2)}, u32[]{:S(2)}) async-start(f32[2,128,16,128]{3,2,0,1:T(8,128)} %copy.121), calls=%async_computation | async-start | bytes 4194304 | tf_op jit(solution)/shard_map/all_to_all | solution.py:92
  112.2 2.2 copy-start.2
  112.2 2.2 copy-start.5
  115.4 1.1 copy-start.10
  120.3 1.3 copy-start.3
  121.7 2.9 collective-permute-start
  121.8 19.5 %copy-start.4 = (f32[2,128,2,128,1]{3,1,0,2,4:T(8,128)S(1)}, f32[2,128,2,128,1]{3,1,0,2,4:T(8,128)}, u32[]{:S(2)}) copy-start(f32[2,128,2,128,1]{3,1,0,2,4:T(8,128)} %constant.112) | copy-start | bytes 786436
  127.0 14.3 %collective-permute-start.1 = (f32[2,4,128,128]{2,3,0,1:T(8,128)}, f32[2,4,128,128]{2,3,0,1:T(8,128)}, u32[]{:S(2)}, u32[]{:S(2)}) collective-permute-start(f32[2,4,128,128]{2,3,0,1:T(8,128)} %constant_dynamic-slice_fusion.1), channel_id=1, source_target_pairs={{0,16},{8,24},{16,0},{24,8},{1,17},{9,25},{17,1},{25,9},{2,18},{10... | collective-permute-start | bytes 1572872 | tf_op jit(solution)/shard_map/ppermute | solution.py:61
  144.6 21.7 %all-to-all-start.2 = ((f32[2,4,128,128]{3,0,1,2:T(2,128)}), f32[2,4,128,128]{3,0,1,2:T(2,128)}, u32[]{:S(2)}, u32[]{:S(2)}) async-start(f32[2,4,128,128]{3,0,1,2:T(2,128)} %copy.137), calls=%async_computation.2 | async-start | bytes 1048576 | tf_op jit(solution)/shard_map/all_to_all | solution.py:69
  166.3 2.7 copy-start.12
  170.4 19.7 %all-to-all-start.3 = ((f32[2,128,4,128]{3,2,0,1:T(4,128)}), f32[2,128,4,128]{3,2,0,1:T(4,128)}, u32[]{:S(2)}, u32[]{:S(2)}) async-start(f32[2,128,4,128]{3,2,0,1:T(4,128)} %copy.140), calls=%async_computation.3 | async-start | bytes 1048576 | tf_op jit(solution)/shard_map/all_to_all | solution.py:76
  175.7 17.0 %copy-start.6 = (f32[2,128,2,128,1]{1,3,0,2,4:T(8,128)S(1)}, f32[2,128,2,128,1]{1,3,0,2,4:T(8,128)}, u32[]{:S(2)}) copy-start(f32[2,128,2,128,1]{1,3,0,2,4:T(8,128)} %constant.110) | copy-start | bytes 786436
  194.3 14.1 %collective-permute-start.2 = (f32[2,4,128,128]{2,3,0,1:T(8,128)S(1)}, f32[2,4,128,128]{2,3,0,1:T(8,128)}, u32[]{:S(2)}, u32[]{:S(2)}) collective-permute-start(f32[2,4,128,128]{2,3,0,1:T(8,128)S(1)} %multiply_add_fusion), channel_id=1, source_target_pairs={{0,16},{8,24},{16,0},{24,8},{1,17},{9,25},{17,1},{25,9},{2,18},{10... | collective-permute-start | bytes 1572872 | tf_op jit(solution)/shard_map/ppermute | solution.py:61
  209.6 2.9 collective-permute-start.3
  213.9 1.0 copy-start.11
  218.1 9.1 %collective-permute-start.4 = (f32[2,16,16,128]{3,2,0,1:T(8,128)S(1)}, f32[2,16,16,128]{3,2,0,1:T(8,128)S(1)}, u32[]{:S(2)}, u32[]{:S(2)}) collective-permute-start(f32[2,16,16,128]{3,2,0,1:T(8,128)S(1)} %get-tuple-element.13), channel_id=1, source_target_pairs={{0,1},{1,0},{2,3},{3,2},{4,5},{5,4},{6,7},{7,6},{8,9},{9,8},{10,11... | collective-permute-start | bytes 786440 | tf_op jit(solution)/shard_map/ppermute | solution.py:23
  218.2 17.4 %collective-permute-start.5 = (f32[2,16,16,128]{3,2,0,1:T(8,128)S(1)}, f32[2,16,16,128]{3,2,0,1:T(8,128)S(1)}, u32[]{:S(2)}, u32[]{:S(2)}) collective-permute-start(f32[2,16,16,128]{3,2,0,1:T(8,128)S(1)} %get-tuple-element.12), channel_id=1, source_target_pairs={{0,2},{1,3},{2,0},{3,1},{4,6},{5,7},{6,4},{7,5},{8,10},{9,11},{10,... | collective-permute-start | bytes 786440 | tf_op jit(solution)/shard_map/ppermute | solution.py:23
  220.3 19.7 %collective-permute-start.6 = (f32[2,16,16,128]{3,2,0,1:T(8,128)S(1)}, f32[2,16,16,128]{3,2,0,1:T(8,128)S(1)}, u32[]{:S(2)}, u32[]{:S(2)}) collective-permute-start(f32[2,16,16,128]{3,2,0,1:T(8,128)S(1)} %get-tuple-element.11), channel_id=1, source_target_pairs={{0,3},{1,2},{2,1},{3,0},{4,7},{5,6},{6,5},{7,4},{8,11},{9,10},{10,... | collective-permute-start | bytes 786440 | tf_op jit(solution)/shard_map/ppermute | solution.py:23
  221.7 18.6 %collective-permute-start.7 = (f32[2,16,16,128]{3,2,0,1:T(8,128)S(1)}, f32[2,16,16,128]{3,2,0,1:T(8,128)S(1)}, u32[]{:S(2)}, u32[]{:S(2)}) collective-permute-start(f32[2,16,16,128]{3,2,0,1:T(8,128)S(1)} %get-tuple-element.10), channel_id=1, source_target_pairs={{0,4},{1,5},{2,6},{3,7},{4,0},{5,1},{6,2},{7,3},{8,12},{9,13},{10,... | collective-permute-start | bytes 786440 | tf_op jit(solution)/shard_map/ppermute | solution.py:23
  222.4 34.9 %collective-permute-start.8 = (f32[2,16,16,128]{3,2,0,1:T(8,128)S(1)}, f32[2,16,16,128]{3,2,0,1:T(8,128)S(1)}, u32[]{:S(2)}, u32[]{:S(2)}) collective-permute-start(f32[2,16,16,128]{3,2,0,1:T(8,128)S(1)} %get-tuple-element.9), channel_id=1, source_target_pairs={{0,5},{1,4},{2,7},{3,6},{4,1},{5,0},{6,3},{7,2},{8,13},{9,12},{10,... | collective-permute-start | bytes 786440 | tf_op jit(solution)/shard_map/ppermute | solution.py:23
  227.0 50.3 %copy-start.7 = (f32[2,128,2,128,1]{3,1,0,4,2:T(8,128)S(1)}, f32[2,128,2,128,1]{3,1,0,4,2:T(8,128)}, u32[]{:S(2)}) copy-start(f32[2,128,2,128,1]{3,1,0,4,2:T(8,128)} %constant.106) | copy-start | bytes 786436
  227.2 37.5 %collective-permute-start.9 = (f32[2,16,16,128]{3,2,0,1:T(8,128)S(1)}, f32[2,16,16,128]{3,2,0,1:T(8,128)S(1)}, u32[]{:S(2)}, u32[]{:S(2)}) collective-permute-start(f32[2,16,16,128]{3,2,0,1:T(8,128)S(1)} %get-tuple-element.8), channel_id=1, source_target_pairs={{0,6},{1,7},{2,4},{3,5},{4,2},{5,3},{6,0},{7,1},{8,14},{9,15},{10,... | collective-permute-start | bytes 786440 | tf_op jit(solution)/shard_map/ppermute | solution.py:23
  235.6 41.5 %collective-permute-start.10 = (f32[2,16,16,128]{3,2,0,1:T(8,128)S(1)}, f32[2,16,16,128]{3,2,0,1:T(8,128)S(1)}, u32[]{:S(2)}, u32[]{:S(2)}) collective-permute-start(f32[2,16,16,128]{3,2,0,1:T(8,128)S(1)} %get-tuple-element.7), channel_id=1, source_target_pairs={{0,7},{1,6},{2,5},{3,4},{4,3},{5,2},{6,1},{7,0},{8,15},{9,14},{10,... | collective-permute-start | bytes 786440 | tf_op jit(solution)/shard_map/ppermute | solution.py:23
  240.1 38.4 %collective-permute-start.11 = (f32[2,16,16,128]{3,2,0,1:T(8,128)S(1)}, f32[2,16,16,128]{3,2,0,1:T(8,128)S(1)}, u32[]{:S(2)}, u32[]{:S(2)}) collective-permute-start(f32[2,16,16,128]{3,2,0,1:T(8,128)S(1)} %get-tuple-element.21), channel_id=1, source_target_pairs={{0,1},{1,0},{2,3},{3,2},{4,5},{5,4},{6,7},{7,6},{8,9},{9,8},{10,11... | collective-permute-start | bytes 786440 | tf_op jit(solution)/shard_map/ppermute | solution.py:23
  240.2 42.3 %collective-permute-start.12 = (f32[2,16,16,128]{3,2,0,1:T(8,128)S(1)}, f32[2,16,16,128]{3,2,0,1:T(8,128)S(1)}, u32[]{:S(2)}, u32[]{:S(2)}) collective-permute-start(f32[2,16,16,128]{3,2,0,1:T(8,128)S(1)} %get-tuple-element.20), channel_id=1, source_target_pairs={{0,2},{1,3},{2,0},{3,1},{4,6},{5,7},{6,4},{7,5},{8,10},{9,11},{10,... | collective-permute-start | bytes 786440 | tf_op jit(solution)/shard_map/ppermute | solution.py:23
  257.3 25.8 %collective-permute-start.13 = (f32[2,16,16,128]{3,2,0,1:T(8,128)S(1)}, f32[2,16,16,128]{3,2,0,1:T(8,128)S(1)}, u32[]{:S(2)}, u32[]{:S(2)}) collective-permute-start(f32[2,16,16,128]{3,2,0,1:T(8,128)S(1)} %get-tuple-element.19), channel_id=1, source_target_pairs={{0,3},{1,2},{2,1},{3,0},{4,7},{5,6},{6,5},{7,4},{8,11},{9,10},{10,... | collective-permute-start | bytes 786440 | tf_op jit(solution)/shard_map/ppermute | solution.py:23
  264.7 32.1 %collective-permute-start.14 = (f32[2,16,16,128]{3,2,0,1:T(8,128)S(1)}, f32[2,16,16,128]{3,2,0,1:T(8,128)S(1)}, u32[]{:S(2)}, u32[]{:S(2)}) collective-permute-start(f32[2,16,16,128]{3,2,0,1:T(8,128)S(1)} %get-tuple-element.18), channel_id=1, source_target_pairs={{0,4},{1,5},{2,6},{3,7},{4,0},{5,1},{6,2},{7,3},{8,12},{9,13},{10,... | collective-permute-start | bytes 786440 | tf_op jit(solution)/shard_map/ppermute | solution.py:23
  277.1 25.3 %collective-permute-start.15 = (f32[2,16,16,128]{3,2,0,1:T(8,128)S(1)}, f32[2,16,16,128]{3,2,0,1:T(8,128)S(1)}, u32[]{:S(2)}, u32[]{:S(2)}) collective-permute-start(f32[2,16,16,128]{3,2,0,1:T(8,128)S(1)} %get-tuple-element.17), channel_id=1, source_target_pairs={{0,5},{1,4},{2,7},{3,6},{4,1},{5,0},{6,3},{7,2},{8,13},{9,12},{10,... | collective-permute-start | bytes 786440 | tf_op jit(solution)/shard_map/ppermute | solution.py:23
  278.4 31.2 %collective-permute-start.16 = (f32[2,16,16,128]{3,2,0,1:T(8,128)S(1)}, f32[2,16,16,128]{3,2,0,1:T(8,128)S(1)}, u32[]{:S(2)}, u32[]{:S(2)}) collective-permute-start(f32[2,16,16,128]{3,2,0,1:T(8,128)S(1)} %get-tuple-element.16), channel_id=1, source_target_pairs={{0,6},{1,7},{2,4},{3,5},{4,2},{5,3},{6,0},{7,1},{8,14},{9,15},{10,... | collective-permute-start | bytes 786440 | tf_op jit(solution)/shard_map/ppermute | solution.py:23
  282.5 32.2 %collective-permute-start.17 = (f32[2,16,16,128]{3,2,0,1:T(8,128)S(1)}, f32[2,16,16,128]{3,2,0,1:T(8,128)S(1)}, u32[]{:S(2)}, u32[]{:S(2)}) collective-permute-start(f32[2,16,16,128]{3,2,0,1:T(8,128)S(1)} %get-tuple-element.15), channel_id=1, source_target_pairs={{0,7},{1,6},{2,5},{3,4},{4,3},{5,2},{6,1},{7,0},{8,15},{9,14},{10,... | collective-permute-start | bytes 786440 | tf_op jit(solution)/shard_map/ppermute | solution.py:23
  316.5 4.5 %copy-start.1 = (f32[16,128,128]{2,1,0:T(8,128)S(1)}, f32[16,128,128]{2,1,0:T(8,128)}, u32[]{:S(2)}) copy-start(f32[16,128,128]{2,1,0:T(8,128)} %param.23) | copy-start | bytes 3145732
